TPU v7x, 32 devices: a whole 2x2x4 slice. The times are simulated.
32 devices in a mesh: gx: 4 (over x, core), gy: 4 (over z), gz: 2 (over y).
Axes of the slice: x: 2, y: 2, z: 4, core: 2. Of those that a mesh axis runs over, the one named last changes fastest.
Arguments:
- unary: bfloat16 [16, 32, 128, 128], P('gx', 'gy', 'gz'), may hold values from -3 to 3
- compat: float32 [6, 128, 128], replicated, may hold values from -2.5 to 2.5
- saved_first: bfloat16 [6, 16, 32, 128, 128], P(None, 'gx', 'gy', 'gz'), may hold values from 0.25 to 4
- saved_second: bfloat16 [6, 16, 32, 128, 128], P(None, 'gx', 'gy', 'gz'), may hold values from 0.25 to 4
- cotangent: float32 [16, 32, 128, 128], P('gx', 'gy', 'gz'), may hold values from -6 to 6
Outputs:
- grad_unary: float32 [16, 32, 128, 128], P('gx', 'gy', 'gz')
- grad_compat: float32 [6, 128, 128], replicated
All inputs are finite; a program needn't handle non-finite values.
Results may differ from a plain program's by a relative error of at most 0.0084.
Values may be sent and summed in bfloat16 or wider, within the bound.
A program may use at most 128 MiB of HBM per device.

v0:
```python
import jax
import jax.numpy as jnp
from jax import lax
from jax.sharding import PartitionSpec as P

OPPOSE = (1, 0, 3, 2, 5, 4)


def extended(cells, sides, width):
    for axis, dim in sides:
        count = lax.axis_size(axis)
        ends = count - 1
        head = lax.slice_in_dim(cells, 0, width, axis=dim)
        tail = lax.slice_in_dim(cells, cells.shape[dim] - width, cells.shape[dim], axis=dim)
        cells = jnp.concatenate(
            [
                lax.ppermute(tail, axis, [(i, (i + 1) % count) for i in range(ends)]),
                cells,
                lax.ppermute(head, axis, [((i + 1) % count, i) for i in range(ends)]),
            ],
            axis=dim,
        )
    return cells


def full_product(fields):
    result = fields[0]
    for index in range(1, 6):
        result = result * fields[index]
    return result


def send_terms(potential, messages, whole, weights_b):
    labels = potential.shape[-1]
    scaled = potential * whole
    hidden = [scaled / messages[OPPOSE[direction]] for direction in range(6)]
    hidden_b = jnp.stack(hidden).astype(jnp.bfloat16)
    outgoing = jnp.einsum(
        "dxyzk,dkl->dxyzl", hidden_b, weights_b, preferred_element_type=jnp.float32
    )
    totals = jnp.sum(outgoing, axis=-1, keepdims=True)
    normal = labels * outgoing / totals
    return (hidden_b, normal, totals)


def trade(low_face, high_face, axis_dim):
    packed = jnp.concatenate([low_face, high_face], axis=axis_dim)
    if axis_dim == 0:
        rims = extended(packed, (("gx", 0),), 1)
    elif axis_dim == 1:
        rims = extended(packed, (("gy", 1),), 1)
    else:
        rims = extended(packed, (("gz", 2),), 1)
    lower = lax.slice_in_dim(rims, 0, 1, axis=axis_dim)
    upper = lax.slice_in_dim(rims, 3, 4, axis=axis_dim)
    return (lower, upper)


def spread(normal_b, lower_edge, upper_edge):
    result = []
    for axis_dim in range(3):
        plus = normal_b[2 * axis_dim]
        minus = normal_b[2 * axis_dim + 1]
        length = plus.shape[axis_dim]
        lower, upper = trade(
            lax.slice_in_dim(minus, 0, 1, axis=axis_dim),
            lax.slice_in_dim(plus, length - 1, length, axis=axis_dim),
            axis_dim,
        )
        ones = jnp.ones_like(lower)
        lower = jnp.where(lower_edge[axis_dim], ones, lower)
        upper = jnp.where(upper_edge[axis_dim], ones, upper)
        result.append(
            jnp.concatenate(
                [lower, lax.slice_in_dim(plus, 0, length - 1, axis=axis_dim)], axis=axis_dim
            )
        )
        result.append(
            jnp.concatenate(
                [lax.slice_in_dim(minus, 1, length, axis=axis_dim), upper], axis=axis_dim
            )
        )
    return result


def gather_back(grad_b):
    result = []
    for axis_dim in range(3):
        plus = grad_b[2 * axis_dim]
        minus = grad_b[2 * axis_dim + 1]
        length = plus.shape[axis_dim]
        lower, upper = trade(
            lax.slice_in_dim(plus, 0, 1, axis=axis_dim),
            lax.slice_in_dim(minus, length - 1, length, axis=axis_dim),
            axis_dim,
        )
        result.append(
            jnp.concatenate(
                [lax.slice_in_dim(plus, 1, length, axis=axis_dim), upper], axis=axis_dim
            )
        )
        result.append(
            jnp.concatenate(
                [lower, lax.slice_in_dim(minus, 0, length - 1, axis=axis_dim)], axis=axis_dim
            )
        )
    return jnp.stack(result).astype(jnp.float32)


def belief_adjoint(potential, arriving, cotangent):
    labels = potential.shape[-1]
    whole = full_product(arriving)
    joint = potential * whole
    summed = jnp.sum(joint, axis=-1, keepdims=True)
    belief = joint / summed
    grad_joint = labels * (cotangent - jnp.sum(cotangent * belief, axis=-1, keepdims=True)) / summed
    grad_potential = grad_joint * whole
    scaled = grad_joint * joint
    grad_arriving = [(scaled / arriving[edge]).astype(jnp.bfloat16) for edge in range(6)]
    return (grad_arriving, grad_potential)


def local_adjoint(grad_normal, normal, totals, hidden_b, weights_b):
    labels = normal.shape[-1]
    inner = jnp.sum(grad_normal * normal, axis=-1, keepdims=True)
    grad_out = (labels / totals * (grad_normal - inner / labels)).astype(jnp.bfloat16)
    grad_weights = jnp.einsum(
        "dxyzk,dxyzl->dkl", hidden_b, grad_out, preferred_element_type=jnp.float32
    )
    grad_hidden = jnp.einsum(
        "dxyzl,dkl->dxyzk", grad_out, weights_b, preferred_element_type=jnp.float32
    )
    return (grad_weights, grad_hidden)


def adjoint_terms(grad_hidden, potential, messages, whole):
    ratios = [grad_hidden[OPPOSE[index]] / messages[index] for index in range(6)]
    total = ratios[0]
    for index in range(1, 6):
        total = total + ratios[index]
    unary_term = whole * total
    scaled = potential * whole
    grad_messages = []
    for edge in range(6):
        partial_sum = None
        for index in range(6):
            if index == edge:
                continue
            partial_sum = ratios[index] if partial_sum is None else partial_sum + ratios[index]
        grad_messages.append((partial_sum * (scaled / messages[edge])).astype(jnp.bfloat16))
    return (unary_term, grad_messages)


def body(unary, compat, saved_first, saved_second, cotangent):
    potential = jnp.exp(unary.astype(jnp.float32))
    weights = jnp.exp(compat)
    weights_b = weights.astype(jnp.bfloat16)
    lower_edge = (lax.axis_index("gx") == 0, lax.axis_index("gy") == 0, lax.axis_index("gz") == 0)
    upper_edge = (
        lax.axis_index("gx") == lax.axis_size("gx") - 1,
        lax.axis_index("gy") == lax.axis_size("gy") - 1,
        lax.axis_index("gz") == lax.axis_size("gz") - 1,
    )
    first = [saved_first[index].astype(jnp.float32) for index in range(6)]
    second = [saved_second[index].astype(jnp.float32) for index in range(6)]
    whole_two = full_product(second)
    hidden_two, normal_two, totals_two = send_terms(potential, second, whole_two, weights_b)
    arriving = spread(
        [normal_two[index].astype(jnp.bfloat16) for index in range(6)], lower_edge, upper_edge
    )
    arriving = [value.astype(jnp.float32) for value in arriving]
    grad_arriving, grad_potential = belief_adjoint(potential, arriving, cotangent)
    grad_normal_two = gather_back(grad_arriving)
    weights_two, grad_hidden_two = local_adjoint(
        grad_normal_two, normal_two, totals_two, hidden_two, weights_b
    )
    unary_two, grad_second = adjoint_terms(grad_hidden_two, potential, second, whole_two)
    grad_potential = grad_potential + unary_two
    whole_one = full_product(first)
    hidden_one, normal_one, totals_one = send_terms(potential, first, whole_one, weights_b)
    grad_normal_one = gather_back(grad_second)
    weights_one, grad_hidden_one = local_adjoint(
        grad_normal_one, normal_one, totals_one, hidden_one, weights_b
    )
    ratios_one = [grad_hidden_one[OPPOSE[index]] / first[index] for index in range(6)]
    total_one = ratios_one[0]
    for index in range(1, 6):
        total_one = total_one + ratios_one[index]
    grad_potential = grad_potential + whole_one * total_one
    grad_unary = potential * grad_potential
    summed = lax.psum(weights_two + weights_one, ("gx", "gy", "gz"))
    grad_compat = weights * summed
    return (grad_unary, grad_compat)


def solution(mesh):
    placed = (
        P("gx", "gy", "gz", None),
        P(),
        P(None, "gx", "gy", "gz", None),
        P(None, "gx", "gy", "gz", None),
        P("gx", "gy", "gz", None),
    )
    return jax.shard_map(
        body,
        mesh=mesh,
        in_specs=placed,
        out_specs=(P("gx", "gy", "gz", None), P()),
        check_vma=False,
    )
```

profile of v0, /device:TPU:0, one launch (start us, length us, event | category | flops | bytes accessed | tf_op | source)
XLA Modules:
  0.0 281.0 jit_solution(6039533829590299076)
XLA Ops:
  7.2 4.7 %bitcast_dynamic-update-slice_fusion.5 = (bf16[6,4,8,64,128]{4,3,2,1,0:T(8,128)(2,1)S(1)}, f32[4,8,64,128]{3,2,1,0:T(8,128)S(1)}, bf16[6,4,8,64,128]{4,3,2,1,0:T(8,128)(2,1)S(1)}, f32[4,8,64,128]{3,2,1,0:T(8,128)S(1)}) fusion(bf16[6,4,8,64,128]{4,3,2,1,0:T(8,128)(2,1)} %param.7, bf16[4,8,64,128]{3,2,1,0:T(8,128)(2,1)} %param.5, ...), kind=kLoop, calls=%fused_computation.152 | loop fusion | flops 7602174 | bytes 9961472
  15.0 1.9 fusion.77
  16.9 2.0 fusion.13
  20.4 1.3 collective-permute-start.3
  22.4 6.2 %collective-permute-start.2 = (bf16[4,1,64,128]{3,2,1,0:T(8,128)(2,1)}, bf16[4,1,64,128]{3,2,1,0:T(8,128)(2,1)}, u32[]{:S(2)}, u32[]{:S(2)}) collective-permute-start(bf16[4,1,64,128]{3,2,1,0:T(8,128)(2,1)} %slice.289), channel_id=1, source_target_pairs={{0,2},{2,4},{4,6},{1,3},{3,5},{5,7},{8,10},{10,12},{12,14},{9,11},... | collective-permute-start | bytes 196616 | tf_op jit(solution)/shard_map/ppermute | solution.py:17
  29.1 1.3 collective-permute-start.5
  31.1 5.1 %collective-permute-start.4 = (bf16[4,8,1,128]{3,2,1,0:T(2,128)(2,1)}, bf16[4,8,1,128]{3,2,1,0:T(2,128)(2,1)S(1)}, u32[]{:S(2)}, u32[]{:S(2)}) collective-permute-start(bf16[4,8,1,128]{3,2,1,0:T(2,128)(2,1)} %slice.295), channel_id=1, source_target_pairs={{0,1},{2,3},{4,5},{6,7},{8,9},{10,11},{12,13},{14,15},{16,17},{18,... | collective-permute-start | bytes 24584 | tf_op jit(solution)/shard_map/ppermute | solution.py:17
  39.6 4.3 %fusion.78 = (f32[6,4,8,64]{3,2,1,0:T(8,128)S(1)}, f32[6,4,8,64,128]{4,3,2,1,0:T(8,128)}) fusion(bf16[6,4,8,64,128]{4,3,2,1,0:T(8,128)(2,1)S(1)} %bitcast_dynamic-update-slice_fusion, bf16[6,128,128,1,1]{2,1,4,3,0:T(8,128)(2,1)S(1)} %fusion.68), kind=kOutput, calls=%fused_computation.182 | convolution fusion | flops 404213760 | bytes 9682944 | tf_op jit(solution)/shard_map/dxyzk,dkl->dxyzl/dot_general | solution.py:38
  46.7 3.3 %collective-permute-start = (bf16[1,8,64,128]{3,2,1,0:T(8,128)(2,1)}, bf16[1,8,64,128]{3,2,1,0:T(8,128)(2,1)S(1)}, u32[]{:S(2)}, u32[]{:S(2)}) collective-permute-start(bf16[1,8,64,128]{3,2,1,0:T(8,128)(2,1)} %get-tuple-element.19), channel_id=1, source_target_pairs={{0,8},{8,16},{16,24},{1,9},{9,17},{17,25},{2,10},{10,18},{18,26},{... | collective-permute-start | bytes 393224 | tf_op jit(solution)/shard_map/ppermute | solution.py:17
  52.7 2.0 fusion.72
  54.8 11.9 %fusion.37 = (bf16[4,8,64,128]{3,2,1,0:T(8,128)(2,1)S(1)}, f32[4,8,64,128]{3,2,1,0:T(8,128)S(1)}, f32[4,8,64,128]{3,2,1,0:T(8,128)}) fusion(bf16[4,8,1,128]{3,2,1,0:T(2,128)(2,1)S(1)} %broadcast_select_fusion.4, bf16[4,8,63,128]{3,2,1,0:T(8,128)(2,1)S(1)} %copy-done.16, f32[4,8,64,128]{3,2,1,0:T(8,128)S(1)} %get-tuple-element.13, ...), kind=kOutput, calls=%fused_computation.75 | output fusion | flops 4196479 | bytes 5775360 | tf_op jit(solution)/shard_map/sub | solution.py:116
  67.5 1.4 collective-permute-start.6
  69.0 4.1 %collective-permute-start.7 = (bf16[1,8,64,128]{3,2,1,0:T(8,128)(2,1)S(1)}, bf16[1,8,64,128]{3,2,1,0:T(8,128)(2,1)S(1)}, u32[]{:S(2)}, u32[]{:S(2)}) collective-permute-start(bf16[1,8,64,128]{3,2,1,0:T(8,128)(2,1)S(1)} %slice.302), channel_id=1, source_target_pairs={{0,8},{8,16},{16,24},{1,9},{9,17},{17,25},{2,10},{10,18},{18,26},{... | collective-permute-start | bytes 393224 | tf_op jit(solution)/shard_map/ppermute | solution.py:17
  73.5 1.4 collective-permute-start.8
  74.9 4.5 %collective-permute-start.9 = (bf16[4,1,64,128]{3,2,1,0:T(8,128)(2,1)S(1)}, bf16[4,1,64,128]{3,2,1,0:T(8,128)(2,1)S(1)}, u32[]{:S(2)}, u32[]{:S(2)}) collective-permute-start(bf16[4,1,64,128]{3,2,1,0:T(8,128)(2,1)S(1)} %slice.306), channel_id=1, source_target_pairs={{0,2},{2,4},{4,6},{1,3},{3,5},{5,7},{8,10},{10,12},{12,14},{9,11},... | collective-permute-start | bytes 196616 | tf_op jit(solution)/shard_map/ppermute | solution.py:17
  79.5 1.3 collective-permute-start.10
  80.8 4.5 %collective-permute-start.11 = (bf16[4,8,1,128]{3,2,1,0:T(2,128)(2,1)S(1)}, bf16[4,8,1,128]{3,2,1,0:T(2,128)(2,1)S(1)}, u32[]{:S(2)}, u32[]{:S(2)}) collective-permute-start(bf16[4,8,1,128]{3,2,1,0:T(2,128)(2,1)S(1)} %slice.310), channel_id=1, source_target_pairs={{0,1},{2,3},{4,5},{6,7},{8,9},{10,11},{12,13},{14,15},{16,17},{18,... | collective-permute-start | bytes 24584 | tf_op jit(solution)/shard_map/ppermute | solution.py:17
  87.0 3.8 %fusion.1 = f32[6,4,8,64]{3,2,1,0:T(8,128)S(1)} fusion(bf16[6,4,8,64,128]{4,3,2,1,0:T(8,128)(2,1)S(1)} %fusion.60, f32[6,4,8,64]{3,2,1,0:T(8,128)S(1)} %get-tuple-element.34, f32[6,4,8,64,128]{4,3,2,1,0:T(8,128)S(1)} %bitcast.354), kind=kLoop, calls=%fused_computation.5 | loop fusion | flops 7852032 | bytes 9535488 | tf_op jit(solution)/shard_map/reduce_sum | solution.py:125
  90.8 5.5 %fusion.79 = f32[6,4,8,64,128]{4,3,2,1,0:T(8,128)S(1)} fusion(bf16[6,128,128,1,1]{2,1,4,3,0:T(8,128)(2,1)S(1)} %fusion.68, bf16[6,4,8,64,128]{4,3,2,1,0:T(8,128)(2,1)S(1)} %fusion.60, f32[6,4,8,64]{3,2,1,0:T(8,128)S(1)} %broadcast_multiply_fusion.1, f32[6,4,8,64]{3,2,1,0:T(8,128)S(1)} %copy-done.21), kind=kOutput, calls=%fused_computation.183 | convolution fusion | flops 408944640 | bytes 9732096 | tf_op jit(solution)/shard_map/dxyzl,dkl->dxyzk/dot_general | solution.py:130
  100.5 2.1 collective-permute-start.13
  102.6 1.6 collective-permute-start.12
  104.2 5.7 %fusion.17 = f32[6,128,128]{2,1,0:T(8,128)S(1)} fusion(bf16[6,4,8,64,128]{4,3,2,1,0:T(8,128)(2,1)S(1)} %copy-done.12, bf16[6,4,8,64,128]{4,3,2,1,0:T(8,128)(2,1)S(1)} %fusion.60, f32[6,4,8,64]{3,2,1,0:T(8,128)S(1)} %broadcast_multiply_fusion.1, f32[6,4,8,64]{3,2,1,0:T(8,128)S(1)} %copy-done.21), kind=kOutput, calls=%fused_computation.67 | convolution fusion | flops 408944640 | bytes 6782976 | tf_op jit(solution)/shard_map/dxyzk,dxyzl->dkl/dot_general | solution.py:127
  110.2 1.3 collective-permute-start.14
  111.5 4.7 %collective-permute-start.15 = (bf16[4,1,64,128]{3,2,1,0:T(8,128)(2,1)S(1)}, bf16[4,1,64,128]{3,2,1,0:T(8,128)(2,1)S(1)}, u32[]{:S(2)}, u32[]{:S(2)}) collective-permute-start(bf16[4,1,64,128]{3,2,1,0:T(8,128)(2,1)S(1)} %slice.324), channel_id=1, source_target_pairs={{0,2},{2,4},{4,6},{1,3},{3,5},{5,7},{8,10},{10,12},{12,14},{9,11},... | collective-permute-start | bytes 196616 | tf_op jit(solution)/shard_map/ppermute | solution.py:17
  116.3 1.3 collective-permute-start.16
  117.6 4.8 %collective-permute-start.17 = (bf16[4,8,1,128]{3,2,1,0:T(2,128)(2,1)S(1)}, bf16[4,8,1,128]{3,2,1,0:T(2,128)(2,1)S(1)}, u32[]{:S(2)}, u32[]{:S(2)}) collective-permute-start(bf16[4,8,1,128]{3,2,1,0:T(2,128)(2,1)S(1)} %slice.328), channel_id=1, source_target_pairs={{0,1},{2,3},{4,5},{6,7},{8,9},{10,11},{12,13},{14,15},{16,17},{18,... | collective-permute-start | bytes 24584 | tf_op jit(solution)/shard_map/ppermute | solution.py:17
  123.9 3.8 %fusion.4 = f32[6,4,8,64]{3,2,1,0:T(8,128)S(1)} fusion(bf16[6,4,8,64,128]{4,3,2,1,0:T(8,128)(2,1)S(1)} %fusion.66, f32[6,4,8,64,128]{4,3,2,1,0:T(8,128)S(1)} %bitcast.356, f32[6,4,8,64]{3,2,1,0:T(8,128)S(1)} %get-tuple-element.37), kind=kLoop, calls=%fused_computation.8 | loop fusion | flops 7852032 | bytes 9535488 | tf_op jit(solution)/shard_map/reduce_sum | solution.py:125
  127.7 6.8 %fusion.80 = f32[6,4,8,64,128]{4,3,2,1,0:T(8,128)} fusion(bf16[6,128,128,1,1]{2,1,4,3,0:T(8,128)(2,1)S(1)} %fusion.68, bf16[6,4,8,64,128]{4,3,2,1,0:T(8,128)(2,1)S(1)} %fusion.66, f32[6,4,8,64]{3,2,1,0:T(8,128)S(1)} %broadcast_multiply_fusion, f32[6,4,8,64]{3,2,1,0:T(8,128)S(1)} %broadcast_divide_fusion), kind=kOutput, calls=%fused_computation.184 | convolution fusion | flops 408944640 | bytes 9732096 | tf_op jit(solution)/shard_map/dxyzl,dkl->dxyzk/dot_general | solution.py:130
  134.5 6.2 %fusion.27 = f32[6,128,128]{2,1,0:T(8,128)} fusion(f32[6,128,128]{2,1,0:T(8,128)S(1)} %fusion.17, bf16[6,4,8,64,128]{4,3,2,1,0:T(8,128)(2,1)S(1)} %copy-done.10, bf16[6,4,8,64,128]{4,3,2,1,0:T(8,128)(2,1)S(1)} %fusion.66, f32[6,4,8,64]{3,2,1,0:T(8,128)S(1)} %broadcast_multiply_fusion, f32[6,4,8,64]{3,2,1,0:T(8,128)S(1)} %broadcast_divide_fusion), kind=kOutput, calls=%fused_computation.69 | convolution fusion | flops 409042944 | bytes 7176192 | tf_op jit(solution)/shard_map/dxyzk,dxyzl->dkl/dot_general | solution.py:127
  140.8 7.4 %fusion.46 = f32[4,8,64,128]{3,2,1,0:T(8,128)} fusion(f32[6,4,8,64,128]{4,3,2,1,0:T(8,128)} %fusion.80, f32[4,8,64,128]{3,2,1,0:T(8,128)} %copy-done.6, f32[4,8,64,128]{3,2,1,0:T(8,128)} %get-tuple-element.36, f32[4,8,64,128]{3,2,1,0:T(8,128)} %copy-done.13, bf16[4,8,64,128]{3,2,1,0:T(8,128)(2,1)} %param.5, f32[4,8,64,128]{3,2,1,0:T(8,128)} %copy-done.7, ...), kind=kLoop, calls=%fused_computation.84 | loop fusion | flops 11010048 | bytes 19398656 | tf_op jit(solution)/shard_map/mul | solution.py:190
  148.2 124.2 %all-reduce.2.cloned.1.call-done = f32[6,128,128]{2,1,0:T(8,128)} async-done(((f32[6,128,128]{2,1,0:T(8,128)}), f32[6,128,128]{2,1,0:T(8,128)}) %all-reduce.2.cloned.1.call-update) | async-done | bytes 393232 | tf_op jit(solution)/shard_map/psum | solution.py:191
  272.4 1.8 exponential_multiply_fusion
  (147 shorter events, 23.7 us)
Async XLA Ops:
  7.2 265.2 %all-reduce.2.cloned.1.call-start = ((), (), s32[]{:S(2)}) async-start(), calls=%async_computation | async-start | bytes 786432 | tf_op jit(solution)/shard_map/psum | solution.py:191
  19.8 19.8 %copy-start.18 = (bf16[4,8,64,128]{3,2,1,0:T(8,128)(2,1)}, bf16[4,8,64,128]{3,2,1,0:T(8,128)(2,1)S(1)}, u32[]{:S(2)}) copy-start(bf16[4,8,64,128]{3,2,1,0:T(8,128)(2,1)S(1)} %get-tuple-element.26) | copy-start | bytes 1572868
  20.4 30.4 %collective-permute-start.3 = (bf16[4,1,64,128]{3,2,1,0:T(8,128)(2,1)}, bf16[4,1,64,128]{3,2,1,0:T(8,128)(2,1)}, u32[]{:S(2)}, u32[]{:S(2)}) collective-permute-start(bf16[4,1,64,128]{3,2,1,0:T(8,128)(2,1)} %slice.293), channel_id=1, source_target_pairs={{2,0},{4,2},{6,4},{3,1},{5,3},{7,5},{10,8},{12,10},{14,12},{11,9},... | collective-permute-start | bytes 196616 | tf_op jit(solution)/shard_map/ppermute | solution.py:19
  22.4 29.3 %collective-permute-start.2 = (bf16[4,1,64,128]{3,2,1,0:T(8,128)(2,1)}, bf16[4,1,64,128]{3,2,1,0:T(8,128)(2,1)}, u32[]{:S(2)}, u32[]{:S(2)}) collective-permute-start(bf16[4,1,64,128]{3,2,1,0:T(8,128)(2,1)} %slice.289), channel_id=1, source_target_pairs={{0,2},{2,4},{4,6},{1,3},{3,5},{5,7},{8,10},{10,12},{12,14},{9,11},... | collective-permute-start | bytes 196616 | tf_op jit(solution)/shard_map/ppermute | solution.py:17
  29.1 17.5 %collective-permute-start.5 = (bf16[4,8,1,128]{3,2,1,0:T(2,128)(2,1)}, bf16[4,8,1,128]{3,2,1,0:T(2,128)(2,1)}, u32[]{:S(2)}, u32[]{:S(2)}) collective-permute-start(bf16[4,8,1,128]{3,2,1,0:T(2,128)(2,1)} %slice.299), channel_id=1, source_target_pairs={{1,0},{3,2},{5,4},{7,6},{9,8},{11,10},{13,12},{15,14},{17,16},{19,... | collective-permute-start | bytes 24584 | tf_op jit(solution)/shard_map/ppermute | solution.py:19
  31.1 19.7 %collective-permute-start.4 = (bf16[4,8,1,128]{3,2,1,0:T(2,128)(2,1)}, bf16[4,8,1,128]{3,2,1,0:T(2,128)(2,1)S(1)}, u32[]{:S(2)}, u32[]{:S(2)}) collective-permute-start(bf16[4,8,1,128]{3,2,1,0:T(2,128)(2,1)} %slice.295), channel_id=1, source_target_pairs={{0,1},{2,3},{4,5},{6,7},{8,9},{10,11},{12,13},{14,15},{16,17},{18,... | collective-permute-start | bytes 24584 | tf_op jit(solution)/shard_map/ppermute | solution.py:17
  36.9 14.8 %collective-permute-start.1 = (bf16[1,8,64,128]{3,2,1,0:T(8,128)(2,1)}, bf16[1,8,64,128]{3,2,1,0:T(8,128)(2,1)}, u32[]{:S(2)}, u32[]{:S(2)}) collective-permute-start(bf16[1,8,64,128]{3,2,1,0:T(8,128)(2,1)} %get-tuple-element.20), channel_id=1, source_target_pairs={{8,0},{16,8},{24,16},{9,1},{17,9},{25,17},{10,2},{18,10},{26,18},{... | collective-permute-start | bytes 393224 | tf_op jit(solution)/shard_map/ppermute | solution.py:19
  43.9 8.8 %copy-start.8 = (bf16[4,8,64,128]{3,2,1,0:T(8,128)(2,1)S(1)}, bf16[4,8,64,128]{3,2,1,0:T(8,128)(2,1)}, u32[]{:S(2)}) copy-start(bf16[4,8,64,128]{3,2,1,0:T(8,128)(2,1)} %param.5) | copy-start | bytes 1572868
  46.6 8.1 %copy-start.16 = (bf16[4,8,63,128]{3,2,1,0:T(8,128)(2,1)S(1)}, bf16[4,8,63,128]{3,2,1,0:T(8,128)(2,1)}, u32[]{:S(2)}) copy-start(bf16[4,8,63,128]{3,2,1,0:T(8,128)(2,1)} %slice.298) | copy-start | bytes 1548292
  46.7 6.0 %collective-permute-start = (bf16[1,8,64,128]{3,2,1,0:T(8,128)(2,1)}, bf16[1,8,64,128]{3,2,1,0:T(8,128)(2,1)S(1)}, u32[]{:S(2)}, u32[]{:S(2)}) collective-permute-start(bf16[1,8,64,128]{3,2,1,0:T(8,128)(2,1)} %get-tuple-element.19), channel_id=1, source_target_pairs={{0,8},{8,16},{16,24},{1,9},{9,17},{17,25},{2,10},{10,18},{18,26},{... | collective-permute-start | bytes 393224 | tf_op jit(solution)/shard_map/ppermute | solution.py:17
  54.7 11.9 %copy-start.13 = (f32[4,8,64,128]{3,2,1,0:T(8,128)}, f32[4,8,64,128]{3,2,1,0:T(8,128)S(1)}, u32[]{:S(2)}) copy-start(f32[4,8,64,128]{3,2,1,0:T(8,128)S(1)} %get-tuple-element.13) | copy-start | bytes 3145732
  54.7 11.9 %copy-start.14 = (bf16[3,8,64,128]{3,2,1,0:T(8,128)(2,1)S(1)}, bf16[3,8,64,128]{3,2,1,0:T(8,128)(2,1)}, u32[]{:S(2)}) copy-start(bf16[3,8,64,128]{3,2,1,0:T(8,128)(2,1)} %get-tuple-element.21) | copy-start | bytes 1179652
  54.7 11.9 %copy-start.15 = (bf16[3,8,64,128]{3,2,1,0:T(8,128)(2,1)S(1)}, bf16[3,8,64,128]{3,2,1,0:T(8,128)(2,1)}, u32[]{:S(2)}) copy-start(bf16[3,8,64,128]{3,2,1,0:T(8,128)(2,1)} %get-tuple-element.22) | copy-start | bytes 1179652
  66.6 20.4 %slice-start = ((s8[6291456]{0:T(1024)(128)(4,1)}), s8[4194304]{0:T(1024)(128)(4,1)S(1)}, s32[]{:S(2)}) async-start(s8[6291456]{0:T(1024)(128)(4,1)} %bitcast.353), calls=%async_computation.1 | async-start | bytes 8388608
  67.5 13.3 %collective-permute-start.6 = (bf16[1,8,64,128]{3,2,1,0:T(8,128)(2,1)S(1)}, bf16[1,8,64,128]{3,2,1,0:T(8,128)(2,1)S(1)}, u32[]{:S(2)}, u32[]{:S(2)}) collective-permute-start(bf16[1,8,64,128]{3,2,1,0:T(8,128)(2,1)S(1)} %slice.301), channel_id=1, source_target_pairs={{8,0},{16,8},{24,16},{9,1},{17,9},{25,17},{10,2},{18,10},{26,18},{... | collective-permute-start | bytes 393224 | tf_op jit(solution)/shard_map/ppermute | solution.py:19
  69.0 16.4 %collective-permute-start.7 = (bf16[1,8,64,128]{3,2,1,0:T(8,128)(2,1)S(1)}, bf16[1,8,64,128]{3,2,1,0:T(8,128)(2,1)S(1)}, u32[]{:S(2)}, u32[]{:S(2)}) collective-permute-start(bf16[1,8,64,128]{3,2,1,0:T(8,128)(2,1)S(1)} %slice.302), channel_id=1, source_target_pairs={{0,8},{8,16},{16,24},{1,9},{9,17},{17,25},{2,10},{10,18},{18,26},{... | collective-permute-start | bytes 393224 | tf_op jit(solution)/shard_map/ppermute | solution.py:17
  73.1 13.9 %slice-start.1 = ((s8[6291456]{0:T(1024)(128)(4,1)}), s8[2097152]{0:T(1024)(128)(4,1)S(1)}, s32[]{:S(2)}) async-start(s8[6291456]{0:T(1024)(128)(4,1)} %bitcast.353), calls=%async_computation.2 | async-start | bytes 4194304
  73.5 12.0 %collective-permute-start.8 = (bf16[4,1,64,128]{3,2,1,0:T(8,128)(2,1)S(1)}, bf16[4,1,64,128]{3,2,1,0:T(8,128)(2,1)S(1)}, u32[]{:S(2)}, u32[]{:S(2)}) collective-permute-start(bf16[4,1,64,128]{3,2,1,0:T(8,128)(2,1)S(1)} %slice.305), channel_id=1, source_target_pairs={{2,0},{4,2},{6,4},{3,1},{5,3},{7,5},{10,8},{12,10},{14,12},{11,9},... | collective-permute-start | bytes 196616 | tf_op jit(solution)/shard_map/ppermute | solution.py:19
  74.9 10.7 %collective-permute-start.9 = (bf16[4,1,64,128]{3,2,1,0:T(8,128)(2,1)S(1)}, bf16[4,1,64,128]{3,2,1,0:T(8,128)(2,1)S(1)}, u32[]{:S(2)}, u32[]{:S(2)}) collective-permute-start(bf16[4,1,64,128]{3,2,1,0:T(8,128)(2,1)S(1)} %slice.306), channel_id=1, source_target_pairs={{0,2},{2,4},{4,6},{1,3},{3,5},{5,7},{8,10},{10,12},{12,14},{9,11},... | collective-permute-start | bytes 196616 | tf_op jit(solution)/shard_map/ppermute | solution.py:17
  79.5 6.2 %collective-permute-start.10 = (bf16[4,8,1,128]{3,2,1,0:T(2,128)(2,1)S(1)}, bf16[4,8,1,128]{3,2,1,0:T(2,128)(2,1)S(1)}, u32[]{:S(2)}, u32[]{:S(2)}) collective-permute-start(bf16[4,8,1,128]{3,2,1,0:T(2,128)(2,1)S(1)} %slice.309), channel_id=1, source_target_pairs={{1,0},{3,2},{5,4},{7,6},{9,8},{11,10},{13,12},{15,14},{17,16},{19,... | collective-permute-start | bytes 24584 | tf_op jit(solution)/shard_map/ppermute | solution.py:19
  80.8 6.0 %collective-permute-start.11 = (bf16[4,8,1,128]{3,2,1,0:T(2,128)(2,1)S(1)}, bf16[4,8,1,128]{3,2,1,0:T(2,128)(2,1)S(1)}, u32[]{:S(2)}, u32[]{:S(2)}) collective-permute-start(bf16[4,8,1,128]{3,2,1,0:T(2,128)(2,1)S(1)} %slice.310), channel_id=1, source_target_pairs={{0,1},{2,3},{4,5},{6,7},{8,9},{10,11},{12,13},{14,15},{16,17},{18,... | collective-permute-start | bytes 24584 | tf_op jit(solution)/shard_map/ppermute | solution.py:17
  99.0 10.9 %copy-start.17 = (bf16[4,8,64,128]{3,2,1,0:T(8,128)(2,1)}, bf16[4,8,64,128]{3,2,1,0:T(8,128)(2,1)S(1)}, u32[]{:S(2)}) copy-start(bf16[4,8,64,128]{3,2,1,0:T(8,128)(2,1)S(1)} %multiply_convert_fusion.5) | copy-start | bytes 1572868
  99.3 24.6 %slice-start.2 = ((s8[6291456]{0:T(1024)(128)(4,1)}), s8[2097152]{0:T(1024)(128)(4,1)S(1)}, s32[]{:S(2)}) async-start(s8[6291456]{0:T(1024)(128)(4,1)} %bitcast.355), calls=%async_computation.3 | async-start | bytes 4194304
  100.5 22.0 %collective-permute-start.13 = (bf16[1,8,64,128]{3,2,1,0:T(8,128)(2,1)S(1)}, bf16[1,8,64,128]{3,2,1,0:T(8,128)(2,1)S(1)}, u32[]{:S(2)}, u32[]{:S(2)}) collective-permute-start(bf16[1,8,64,128]{3,2,1,0:T(8,128)(2,1)S(1)} %slice.320), channel_id=1, source_target_pairs={{0,8},{8,16},{16,24},{1,9},{9,17},{17,25},{2,10},{10,18},{18,26},{... | collective-permute-start | bytes 393224 | tf_op jit(solution)/shard_map/ppermute | solution.py:17
  102.6 21.2 %slice-start.3 = ((s8[6291456]{0:T(1024)(128)(4,1)}), s8[4194304]{0:T(1024)(128)(4,1)S(1)}, s32[]{:S(2)}) async-start(s8[6291456]{0:T(1024)(128)(4,1)} %bitcast.355), calls=%async_computation.4 | async-start | bytes 8388608
  102.6 15.0 %collective-permute-start.12 = (bf16[1,8,64,128]{3,2,1,0:T(8,128)(2,1)S(1)}, bf16[1,8,64,128]{3,2,1,0:T(8,128)(2,1)S(1)}, u32[]{:S(2)}, u32[]{:S(2)}) collective-permute-start(bf16[1,8,64,128]{3,2,1,0:T(8,128)(2,1)S(1)} %slice.319), channel_id=1, source_target_pairs={{8,0},{16,8},{24,16},{9,1},{17,9},{25,17},{10,2},{18,10},{26,18},{... | collective-permute-start | bytes 393224 | tf_op jit(solution)/shard_map/ppermute | solution.py:19
  109.9 12.5 %slice-start.4 = ((bf16[4,8,64,128]{3,2,1,0:T(8,128)(2,1)}), bf16[3,8,64,128]{3,2,1,0:T(8,128)(2,1)S(1)}, s32[]{:S(2)}) async-start(bf16[4,8,64,128]{3,2,1,0:T(8,128)(2,1)} %copy-done.17), calls=%async_computation.5 | async-start | bytes 786432 | tf_op jit(solution)/shard_map/slice | solution.py:99
  110.2 12.3 %collective-permute-start.14 = (bf16[4,1,64,128]{3,2,1,0:T(8,128)(2,1)S(1)}, bf16[4,1,64,128]{3,2,1,0:T(8,128)(2,1)S(1)}, u32[]{:S(2)}, u32[]{:S(2)}) collective-permute-start(bf16[4,1,64,128]{3,2,1,0:T(8,128)(2,1)S(1)} %slice.323), channel_id=1, source_target_pairs={{2,0},{4,2},{6,4},{3,1},{5,3},{7,5},{10,8},{12,10},{14,12},{11,9},... | collective-permute-start | bytes 196616 | tf_op jit(solution)/shard_map/ppermute | solution.py:19
  111.5 11.1 %collective-permute-start.15 = (bf16[4,1,64,128]{3,2,1,0:T(8,128)(2,1)S(1)}, bf16[4,1,64,128]{3,2,1,0:T(8,128)(2,1)S(1)}, u32[]{:S(2)}, u32[]{:S(2)}) collective-permute-start(bf16[4,1,64,128]{3,2,1,0:T(8,128)(2,1)S(1)} %slice.324), channel_id=1, source_target_pairs={{0,2},{2,4},{4,6},{1,3},{3,5},{5,7},{8,10},{10,12},{12,14},{9,11},... | collective-permute-start | bytes 196616 | tf_op jit(solution)/shard_map/ppermute | solution.py:17
  116.3 6.4 %collective-permute-start.16 = (bf16[4,8,1,128]{3,2,1,0:T(2,128)(2,1)S(1)}, bf16[4,8,1,128]{3,2,1,0:T(2,128)(2,1)S(1)}, u32[]{:S(2)}, u32[]{:S(2)}) collective-permute-start(bf16[4,8,1,128]{3,2,1,0:T(2,128)(2,1)S(1)} %slice.327), channel_id=1, source_target_pairs={{1,0},{3,2},{5,4},{7,6},{9,8},{11,10},{13,12},{15,14},{17,16},{19,... | collective-permute-start | bytes 24584 | tf_op jit(solution)/shard_map/ppermute | solution.py:19
  117.6 6.0 %collective-permute-start.17 = (bf16[4,8,1,128]{3,2,1,0:T(2,128)(2,1)S(1)}, bf16[4,8,1,128]{3,2,1,0:T(2,128)(2,1)S(1)}, u32[]{:S(2)}, u32[]{:S(2)}) collective-permute-start(bf16[4,8,1,128]{3,2,1,0:T(2,128)(2,1)S(1)} %slice.328), channel_id=1, source_target_pairs={{0,1},{2,3},{4,5},{6,7},{8,9},{10,11},{12,13},{14,15},{16,17},{18,... | collective-permute-start | bytes 24584 | tf_op jit(solution)/shard_map/ppermute | solution.py:17
  140.8 131.6 %copy-start.20 = (f32[6,128,128]{2,1,0:T(8,128)S(1)}, f32[6,128,128]{2,1,0:T(8,128)}, u32[]{:S(2)}) copy-start(f32[6,128,128]{2,1,0:T(8,128)} %param.6) | copy-start | bytes 1179652
  (15 other events, 57.0 us)
Sparse Core Ops, SparseCore 0:
  140.9 131.4 all-reduce.1
where the time goes:
time: 282 us; the launch traced here: 281 us
  waiting for transfers between devices  126 us (45%)
  starting transfers between devices  51.6 us (18%)
  other arithmetic  48.6 us (17%)
  matrix products  30.4 us (11%)
  between operations  15.1 us (5%)
  local copies, waits for them, and re-layouts  9.25 us (3%)
    psum x1, waiting for transfers between devices, body(): summed = lax.psum(weights_two + weights_one, ('gx', 'gy', 'gz'))  124 us
    ppermute x9, starting transfers between devices, extended(): lax.ppermute(tail, axis, [(i, (i + 1) % count) for i in range(ends)])  39.4 us
    dot_general x2, matrix products, local_adjoint(): jnp.einsum('dxyzl,dkl->dxyzk', grad_out, weights_b, preferred_element_typ...  12.3 us
    ppermute x9, starting transfers between devices, extended(): lax.ppermute(head, axis, [((i + 1) % count, i) for i in range(ends)])  12.1 us
    dot_general x2, matrix products, local_adjoint(): jnp.einsum('dxyzk,dxyzl->dkl', hidden_b, grad_out, preferred_element_type...  11.9 us
    sub x1, other arithmetic, belief_adjoint(): cotangent - jnp.sum(cotangent * belief, axis=-1, keepdims=True)  11.9 us
    reduce_sum x2, other arithmetic, local_adjoint(): inner = jnp.sum(grad_normal * normal, axis=-1, keepdims=True)  7.55 us
    unnamed x21, other arithmetic  7.39 us
  transfers between devices with their start and end apart: 19, of which 3 were waited for; matrix products, arithmetic and copies ran while one was open for 10% of the time, Pallas kernels for 0%

commit v1 on v0

v1 whole, which is shorter than its diff:
```python
import functools

import jax
import jax.numpy as jnp
from jax import lax
from jax.experimental import pallas as pl
from jax.experimental.pallas import tpu as pltpu
from jax.sharding import PartitionSpec as P

OPPOSE = (1, 0, 3, 2, 5, 4)
AXES = ("gx", "gy", "gz")
MESH = pl.DeviceIdType.MESH
F32 = jnp.float32
BF16 = jnp.bfloat16
CHUNK = 16


def recip(value):
    guess = pl.reciprocal(value, approx=True)
    return guess * (2.0 - value * guess)


def leave_one_out(start, fields):
    before = [start]
    for index in range(5):
        before.append(before[-1] * fields[index])
    after = fields[5]
    result = [None] * 6
    result[5] = before[5]
    for index in range(4, -1, -1):
        result[index] = before[index] * after
        if index:
            after = after * fields[index]
    return result


class Halo:
    def __init__(self, x_ref, y_ref, z_ref, zhalo_ref, zsend_ref, forward, shape):
        self.x, self.y, self.z, self.zhalo, self.zsend = x_ref, y_ref, z_ref, zhalo_ref, zsend_ref
        self.shape = shape
        self.step = [(-1 if d % 2 == 0 else 1) * (1 if forward else -1) for d in range(6)]

    def own(self, d):
        return 1 if self.step[d] < 0 else 0

    def read(self, d):
        return 0 if self.step[d] < 0 else 1

    def at_own(self, d, x, y):
        if d < 2:
            return self.x.at[d, x + self.own(d), y]
        if d < 4:
            return self.y.at[d - 2, x, y + self.own(d)]
        return self.z.at[d - 4, x, y]

    def at_shifted(self, d, x, y):
        if d < 2:
            return self.x.at[d, x + self.read(d), y]
        return self.y.at[d - 2, x, y + self.read(d)]

    def halo(self, d):
        X, Y, Z, L = self.shape
        if d < 2:
            return self.x.at[d, 0 if self.step[d] < 0 else X]
        if d < 4:
            return self.y.at[d - 2, :, 0 if self.step[d] < 0 else Y]
        return self.zhalo.at[d - 4]

    def face(self, d):
        X, Y, Z, L = self.shape
        if d < 2:
            return self.x.at[d, X if self.step[d] < 0 else 0]
        if d < 4:
            return self.y.at[d - 2, :, Y if self.step[d] < 0 else 0]
        return self.zsend.at[d - 4]


def kernel(
    sizes, scatter, other,
    unary_h, compat, first_h, second_h, cot_h,
    out_h, grad_compat,
    unary, first, second, cot, phi, out, hb, inv, hidden_grad, acc, psib, wide,
    nx, ny, nz, nzs, nzh, nzo, ax, ay, az, azh, azo, bx, by, bz, bzh, bzo,
    rs_src, rs_recv, os_buf, ag_buf,
    in_sem, send_sem, recv_sem, rs_send, rs_recv_sem, os_send, os_recv_sem, ag_send, ag_recv_sem,
):
    X, Y, Z, L = shape = phi.shape
    me = {axis: lax.axis_index(axis) for axis in AXES}

    def target(**changed):
        return tuple(changed.get(axis, me[axis]) for axis in AXES)

    inner_count = sizes[scatter[1]]
    group = sizes[scatter[0]] * inner_count
    mine = me[scatter[0]] * inner_count + me[scatter[1]]
    others = sizes[other]
    rows = 6 * L // group

    def member(index):
        return target(**{scatter[0]: index // inner_count, scatter[1]: index % inner_count})

    loads = [
        pltpu.make_async_copy(src, dst, in_sem.at[i])
        for i, (src, dst) in enumerate(
            ((unary_h, unary), (second_h, second), (cot_h, cot), (first_h, first))
        )
    ]
    for load in loads:
        load.start()

    barrier = pltpu.get_barrier_semaphore()
    for k in range(1, group):
        pl.semaphore_signal(barrier, inc=1, device_id=member((mine + k) % group), device_id_type=MESH)
    for k in range(1, others):
        pl.semaphore_signal(
            barrier, inc=1, device_id=target(**{other: (me[other] + k) % others}), device_id_type=MESH
        )

    for d in range(6):
        rounded = jnp.exp(compat[d]).astype(BF16)
        psib[d] = rounded
        wide[d, :, :L] = rounded
        sums = jnp.sum(rounded.astype(F32), axis=1, keepdims=True)
        wide[d, :, L:] = jnp.broadcast_to(sums, (L, L)).astype(BF16)

    N = Halo(nx, ny, nz, nzh, nzo, True, shape)
    A = Halo(ax, ay, az, azh, azo, False, shape)
    B = Halo(bx, by, bz, bzh, bzo, False, shape)

    def exchange(field, number):
        plan = []
        for d in range(6):
            axis = AXES[d // 2]
            count = sizes[axis]
            place = me[axis]
            up = field.step[d] < 0
            goal = place + 1 if up else place - 1
            sends = place < count - 1 if up else place > 0
            gets = place > 0 if up else place < count - 1
            copy = pltpu.make_async_remote_copy(
                src_ref=field.face(d),
                dst_ref=field.halo(d),
                send_sem=send_sem.at[number, d],
                recv_sem=recv_sem.at[number, d],
                device_id=target(**{axis: goal}),
                device_id_type=MESH,
            )
            plan.append((sends, gets, copy))
        return plan

    def start(plan, field, value):
        for d, (sends, gets, copy) in enumerate(plan):
            @pl.when(sends)
            def _():
                copy.start()

            @pl.when(jnp.logical_not(gets))
            def _():
                spot = field.halo(d)
                spot[...] = jnp.full(spot.shape, value, spot.dtype)

    def wait_recv(plan):
        for sends, gets, copy in plan:
            @pl.when(gets)
            def _():
                copy.wait_recv()

    def wait_send(plan):
        for sends, gets, copy in plan:
            @pl.when(sends)
            def _():
                copy.wait_send()

    def columns(lo, hi, step):
        def one(i, carry):
            step(i // Y, i % Y)
            return carry

        lax.fori_loop(lo * Y, hi * Y, one, 0)

    def planes(lo, hi, step):
        def one(x, carry):
            step(x)
            return carry

        lax.fori_loop(lo, hi, one, 0)

    cuts = [pl.ds(c * CHUNK, CHUNK) for c in range(Z // CHUNK)]
    last = len(cuts) - 1

    def send_terms(messages, shifted):
        def hidden(x, y):
            for cut in cuts:
                if shifted:
                    potential = jnp.exp(unary[x, y, cut].astype(F32))
                    phi[x, y, cut] = potential
                else:
                    potential = phi[x, y, cut]
                fields = [messages[e, x, y, cut].astype(F32) for e in range(6)]
                products = leave_one_out(potential, fields)
                for e in range(6):
                    hb[OPPOSE[e], x, y, cut] = products[e].astype(BF16)

        columns(0, X, hidden)

        def outgoing(x):
            for d in range(6):
                both = jnp.dot(
                    hb[d, x].reshape(Y * Z, L), wide[d], preferred_element_type=F32
                )
                scale = L * recip(both[:, L:])
                inv[d, x] = scale.reshape(Y, Z, L)
                normal = (both[:, :L] * scale).reshape(Y, Z, L)
                if d < 2:
                    nx[d, x + N.own(d)] = normal.astype(BF16)
                elif d < 4:
                    ny[d - 2, x, pl.ds(N.own(d), Y)] = normal.astype(BF16)
                else:
                    nz[d - 4, x] = normal.astype(BF16)
                    if shifted:
                        for y in range(Y):
                            edge = Z - 1 if d == 4 else 0
                            nzo[d - 4, pl.ds(x * Y + y, 1)] = normal[y, edge:edge + 1]
                            nzs[d - 4, x, y] = pltpu.roll(
                                normal[y], 1 if d == 4 else Z - 1, 0
                            ).astype(BF16)

        planes(0, X, outgoing)

    def belief(x, y):
        spot = pl.ds(x * Y + y, 1)
        for c, cut in enumerate(cuts):
            fields = [N.at_shifted(d, x, y)[cut].astype(F32) for d in range(4)]
            row = lax.broadcasted_iota(jnp.int32, (CHUNK, L), 0)
            low = nzs[0, x, y, cut].astype(F32)
            if c == 0:
                low = jnp.where(row == 0, nzh[0, spot].astype(BF16).astype(F32), low)
            high = nzs[1, x, y, cut].astype(F32)
            if c == last:
                high = jnp.where(row == CHUNK - 1, nzh[1, spot].astype(BF16).astype(F32), high)
            fields += [low, high]
            before = [phi[x, y, cut]]
            for e in range(6):
                before.append(before[-1] * fields[e])
            joint = before[6]
            target_grad = cot[x, y, cut]
            scale = recip(jnp.sum(joint, axis=-1, keepdims=True))
            mean = jnp.sum(target_grad * joint, axis=-1, keepdims=True) * scale
            grad = (target_grad - mean) * (L * scale)
            out[x, y, cut] = grad * joint
            after = grad
            for e in range(5, -1, -1):
                value = before[e] * after
                A.at_own(e, x, y)[cut] = value.astype(BF16)
                if e == 4 and c == 0:
                    azo[0, spot] = value[0:1]
                if e == 5 and c == last:
                    azo[1, spot] = value[CHUNK - 1:CHUNK]
                after = after * fields[e]

    def grad_out(field):
        def one(x, y):
            row = lax.broadcasted_iota(jnp.int32, (Z, L), 0)
            spot = pl.ds(x * Y + y, 1)
            for d in range(6):
                if d < 4:
                    grad = field.at_shifted(d, x, y)[...].astype(F32)
                else:
                    value = field.z[d - 4, x, y].astype(F32)
                    halo = field.zhalo[d - 4, spot]
                    if d == 4:
                        grad = jnp.where(row == Z - 1, halo, pltpu.roll(value, Z - 1, 0))
                    else:
                        grad = jnp.where(row == 0, halo, pltpu.roll(value, 1, 0))
                place = N.at_own(d, x, y)
                inner = jnp.sum(grad * place[...].astype(F32), axis=-1, keepdims=True) * (1.0 / L)
                place[...] = (inv[d, x, y] * (grad - inner)).astype(BF16)

        return one

    def go_plane(d, x):
        if d < 2:
            value = nx[d, x + N.own(d)]
        elif d < 4:
            value = ny[d - 2, x, pl.ds(N.own(d), Y)]
        else:
            value = nz[d - 4, x]
        return value.reshape(Y * Z, L)

    def weight_terms(x):
        for d in range(6):
            acc[d] += lax.dot_general(
                hb[d, x].reshape(Y * Z, L), go_plane(d, x), (((0,), (0,)), ((), ())),
                preferred_element_type=F32,
            )

    def hidden_terms(x):
        for d in range(6):
            hidden_grad[d] = lax.dot_general(
                go_plane(d, x), psib[d], (((1,), (1,)), ((), ())), preferred_element_type=F32
            ).reshape(Y, Z, L)

    def adjoint(messages, field):
        def one(x, y):
            spot = pl.ds(x * Y + y, 1)
            for c, cut in enumerate(cuts):
                fields = [messages[e, x, y, cut].astype(F32) for e in range(6)]
                grads = [hidden_grad[OPPOSE[e], y, cut] for e in range(6)]
                before = [phi[x, y, cut]]
                slope = [None]
                for e in range(6):
                    part = before[e] * grads[e]
                    slope.append(part if e == 0 else slope[e] * fields[e] + part)
                    before.append(before[e] * fields[e] if e < 5 else None)
                out[x, y, cut] += slope[6]
                if field is None:
                    continue
                after, fall = None, None
                for e in range(5, -1, -1):
                    if e == 5:
                        value = slope[5]
                        after, fall = fields[5], grads[5]
                    else:
                        value = before[e] * fall
                        if e:
                            value = value + slope[e] * after
                            fall = fall * fields[e] + after * grads[e]
                            after = after * fields[e]
                    field.at_own(e, x, y)[cut] = value.astype(BF16)
                    if e == 4 and c == 0:
                        field.zsend[0, spot] = value[0:1]
                    if e == 5 and c == last:
                        field.zsend[1, spot] = value[CHUNK - 1:CHUNK]

        return one

    loads[0].wait()
    loads[1].wait()
    send_terms(second, True)
    pl.semaphore_wait(barrier, group + others - 2)
    one = exchange(N, 0)
    start(one, N, 1.0)
    acc[...] = jnp.zeros_like(acc)
    loads[2].wait()
    wait_recv(one)
    columns(0, X, belief)
    two = exchange(A, 1)
    start(two, A, 0.0)
    wait_send(one)
    wait_recv(two)

    def second_back(x):
        each = grad_out(A)
        lax.fori_loop(0, Y, lambda y, carry: (each(x, y), carry)[1], 0)
        weight_terms(x)
        hidden_terms(x)
        combine = adjoint(second, B)
        lax.fori_loop(0, Y, lambda y, carry: (combine(x, y), carry)[1], 0)

    planes(0, X, second_back)
    three = exchange(B, 2)
    start(three, B, 0.0)
    wait_send(two)

    loads[3].wait()
    send_terms(first, False)
    wait_recv(three)
    columns(0, X, grad_out(B))
    planes(0, X, weight_terms)
    wait_send(three)

    def first_back(x):
        hidden_terms(x)
        combine = adjoint(first, None)
        lax.fori_loop(0, Y, lambda y, carry: (combine(x, y), carry)[1], 0)

    rs_src[...] = acc[...].reshape(group, rows, L).astype(BF16)
    scatters = []
    for k in range(1, group):
        goal = (mine + k) % group
        scatters.append(
            pltpu.make_async_remote_copy(
                src_ref=rs_src.at[goal], dst_ref=rs_recv.at[k - 1],
                send_sem=rs_send.at[k - 1], recv_sem=rs_recv_sem.at[k - 1],
                device_id=member(goal), device_id_type=MESH,
            )
        )
    for copy in scatters:
        copy.start()
    planes(0, X // 2, first_back)
    total = rs_src[mine].astype(F32)
    for k, copy in enumerate(scatters):
        copy.wait_recv()
        total = total + rs_recv[k].astype(F32)
    os_buf[me[other]] = total.astype(BF16)
    trades = []
    for k in range(1, others):
        goal = (me[other] + k) % others
        source = (me[other] + others - k) % others
        here = pltpu.make_async_remote_copy(
            src_ref=os_buf.at[me[other]], dst_ref=os_buf.at[me[other]],
            send_sem=os_send.at[k - 1], recv_sem=os_recv_sem.at[k - 1],
            device_id=target(**{other: goal}), device_id_type=MESH,
        )
        trades.append(here)
    for copy in trades:
        copy.start()
    planes(X // 2, X // 2 + X // 4, first_back)
    for copy in trades:
        copy.wait_recv()
    total = os_buf[0].astype(F32)
    for k in range(1, others):
        total = total + os_buf[k].astype(F32)
    ag_buf[mine] = total.astype(BF16)
    gathers = []
    for k in range(1, group):
        gathers.append(
            pltpu.make_async_remote_copy(
                src_ref=ag_buf.at[mine], dst_ref=ag_buf.at[mine],
                send_sem=ag_send.at[k - 1], recv_sem=ag_recv_sem.at[k - 1],
                device_id=member((mine + k) % group), device_id_type=MESH,
            )
        )
    for copy in gathers:
        copy.start()
    planes(X // 2 + X // 4, X, first_back)
    store = pltpu.make_async_copy(out, out_h, in_sem.at[4])
    store.start()
    for copy in gathers:
        copy.wait_recv()
    grad_compat[...] = jnp.exp(compat[...]) * ag_buf[...].astype(F32).reshape(6, L, L)
    for copy in scatters + trades + gathers:
        copy.wait_send()
    store.wait()


def body(sizes, unary, compat, saved_first, saved_second, cotangent):
    X, Y, Z, L = unary.shape
    scatter, other = ("gx", "gz"), "gy"
    if (6 * L) % (16 * sizes["gx"] * sizes["gz"]):
        scatter, other = ("gy", "gz"), "gx"
    group = sizes[scatter[0]] * sizes[scatter[1]]
    others = sizes[other]
    rows = 6 * L // group
    field = (X, Y, Z, L)

    def halo_set(extra):
        return [
            pltpu.VMEM((2, X + 1, Y, Z, L), BF16),
            pltpu.VMEM((2, X, Y + 1, Z, L), BF16),
            pltpu.VMEM((2, X, Y, Z, L), BF16),
        ] + extra + [pltpu.VMEM((2, X * Y, L), F32), pltpu.VMEM((2, X * Y, L), F32)]

    dma = pltpu.SemaphoreType.DMA
    return pl.pallas_call(
        functools.partial(kernel, sizes, scatter, other),
        out_shape=(
            jax.ShapeDtypeStruct(field, F32),
            jax.ShapeDtypeStruct((6, L, L), F32),
        ),
        in_specs=[
            pl.BlockSpec(memory_space=pl.ANY),
            pl.BlockSpec(memory_space=pltpu.VMEM),
            pl.BlockSpec(memory_space=pl.ANY),
            pl.BlockSpec(memory_space=pl.ANY),
            pl.BlockSpec(memory_space=pl.ANY),
        ],
        out_specs=(pl.BlockSpec(memory_space=pl.ANY), pl.BlockSpec(memory_space=pltpu.VMEM)),
        scratch_shapes=[
            pltpu.VMEM(field, BF16),
            pltpu.VMEM((6,) + field, BF16),
            pltpu.VMEM((6,) + field, BF16),
            pltpu.VMEM(field, F32),
            pltpu.VMEM(field, F32),
            pltpu.VMEM(field, F32),
            pltpu.VMEM((6,) + field, BF16),
            pltpu.VMEM((6,) + field, F32),
            pltpu.VMEM((6, Y, Z, L), F32),
            pltpu.VMEM((6, L, L), F32),
            pltpu.VMEM((6, L, L), BF16),
            pltpu.VMEM((6, L, 2 * L), BF16),
        ]
        + halo_set([pltpu.VMEM((2, X, Y, Z, L), BF16)])
        + halo_set([])
        + halo_set([])
        + [
            pltpu.VMEM((group, rows, L), BF16),
            pltpu.VMEM((group - 1, rows, L), BF16),
            pltpu.VMEM((others, rows, L), BF16),
            pltpu.VMEM((group, rows, L), BF16),
            dma((5,)),
            dma((3, 6)),
            dma((3, 6)),
            dma((group - 1,)),
            dma((group - 1,)),
            dma((others - 1,)),
            dma((others - 1,)),
            dma((group - 1,)),
            dma((group - 1,)),
        ],
        compiler_params=pltpu.CompilerParams(
            collective_id=0, has_side_effects=True, vmem_limit_bytes=64 * 1024 * 1024 - 65536
        ),
    )(unary, compat, saved_first, saved_second, cotangent)


def solution(mesh):
    sizes = dict(mesh.shape)
    placed = (
        P("gx", "gy", "gz", None),
        P(),
        P(None, "gx", "gy", "gz", None),
        P(None, "gx", "gy", "gz", None),
        P("gx", "gy", "gz", None),
    )
    return jax.shard_map(
        functools.partial(body, sizes),
        mesh=mesh,
        in_specs=placed,
        out_specs=(P("gx", "gy", "gz", None), P()),
        check_vma=False,
    )
```

time: 282 us -> 57.8 us (0.20)
  waiting for transfers between devices: 126 us -> 0 us
  Pallas kernels: 0 us -> 52.9 us
  starting transfers between devices: 51.6 us -> 0 us
  other arithmetic: 48.6 us -> 0 us
  matrix products: 30.4 us -> 0 us
  between operations: 15.1 us -> 0.64 us
  local copies, waits for them, and re-layouts: 9.25 us -> 4.07 us
    psum x1 -> x0, waiting for transfers between devices: 124 us -> none  [body(): summed = lax.psum(weights_two + weights_one, ('gx', 'gy', 'gz'))]
    pallas_call x0 -> x1, Pallas kernels: none -> 52.9 us  [body(): pl.pallas_call(functools.partial(kernel, sizes, scatter, other), out_shap...]
    ppermute x18 -> x0, starting transfers between devices: 51.6 us -> none  [the longest x9 39.4 us: extended(): lax.ppermute(tail, axis, [(i, (i + 1) % count) for i in range(ends)])]
    dot_general x6 -> x0, matrix products: 30.4 us -> none  [the longest x2 12.3 us: local_adjoint(): jnp.einsum('dxyzl,dkl->dxyzk', grad_out, weights_b, preferred_element_typ...]
    sub x1 -> x0, other arithmetic: 11.9 us -> none  [belief_adjoint(): cotangent - jnp.sum(cotangent * belief, axis=-1, keepdims=True)]
    reduce_sum x3 -> x0, other arithmetic: 9.56 us -> none  [the longest x2 7.55 us: local_adjoint(): inner = jnp.sum(grad_normal * normal, axis=-1, keepdims=True)]
    mul x2 -> x0, other arithmetic: 9.17 us -> none  [the longest x1 7.37 us: body(): grad_unary = potential * grad_potential]
    unnamed x21 -> x0, other arithmetic: 7.39 us -> none
  transfers between devices with their start and end apart: 19 -> 0, of which waited for: 3 -> 0; matrix products, arithmetic and copies ran while one was open for 10% -> 0% of each run, Pallas kernels for 0% -> 0%
where the time goes in v1:
time: 57.8 us; the launch traced here: 57.6 us
  Pallas kernels  52.9 us (92%)
  local copies, waits for them, and re-layouts  4.07 us (7%)
  between operations  0.64 us (1%)
    pallas_call x1, Pallas kernels, body(): pl.pallas_call(functools.partial(kernel, sizes, scatter, other), out_shap...  52.9 us
    unnamed x2, local copies, waits for them, and re-layouts  4.07 us

profile of v1, /device:TPU:0, one launch (start us, length us, event | category | flops | bytes accessed | tf_op | source)
XLA Modules:
  0.0 57.6 jit_solution(7655019904287440051)
XLA Ops:
  0.6 52.9 %shard_map.68 = (f32[4,8,64,128]{3,2,1,0:T(8,128)}, f32[6,128,128]{2,1,0:T(8,128)}) custom-call(bf16[4,8,64,128]{3,2,1,0:T(8,128)(2,1)} %unary_h.1, f32[6,128,128]{2,1,0:T(8,128)} %compat.1, bf16[6,4,8,64,128]{4,3,2,1,0:T(8,128)(2,1)} %first_h.1, bf16[6,4,8,64,128]{4,3,2,1,0:T(8,128)(2,1)} %second_h.1, f32[4,8,64,128]{3,2,1,0:T(8,128)} %cot_h.1), custom_call_target="tpu_custom_call" | custom-call | tf_op jit(solution)/shard_map/pallas_call | solution.py:455
  53.5 2.3 %copy.9 = f32[4,8,64,128]{3,2,1,0:T(8,128)} copy(f32[4,8,64,128]{3,2,1,0:T(8,128)} %get-tuple-element.4) | data formatting | bytes 2097152
  55.8 1.8 %copy.10 = f32[6,128,128]{2,1,0:T(8,128)} copy(f32[6,128,128]{2,1,0:T(8,128)} %get-tuple-element.5) | data formatting | bytes 786432

commit v2 on v1

--- a/solution.py
+++ b/solution.py
@@ -58,6 +58,14 @@
             return self.x.at[d, x + self.read(d), y]
         return self.y.at[d - 2, x, y + self.read(d)]
 
+    def plane(self, d, x):
+        X, Y, Z, L = self.shape
+        if d < 2:
+            return self.x.at[d, x + self.own(d)]
+        if d < 4:
+            return self.y.at[d - 2, x, pl.ds(self.own(d), Y)]
+        return self.z.at[d - 4, x]
+
     def halo(self, d):
         X, Y, Z, L = self.shape
         if d < 2:
@@ -75,14 +83,26 @@
         return self.zsend.at[d - 4]
 
 
+class Flat:
+    def __init__(self, ref):
+        self.ref = ref
+
+    def at_own(self, d, x, y):
+        return self.ref.at[d, x, y]
+
+    def plane(self, d, x):
+        return self.ref.at[d, x]
+
+
 def kernel(
-    sizes, scatter, other,
+    early, sizes, scatter, other,
     unary_h, compat, first_h, second_h, cot_h,
     out_h, grad_compat,
     unary, first, second, cot, phi, out, hb, inv, hidden_grad, acc, psib, wide,
     nx, ny, nz, nzs, nzh, nzo, ax, ay, az, azh, azo, bx, by, bz, bzh, bzo,
-    rs_src, rs_recv, os_buf, ag_buf,
+    rs_src, rs_recv, os_buf, ag_buf, mean,
     in_sem, send_sem, recv_sem, rs_send, rs_recv_sem, os_send, os_recv_sem, ag_send, ag_recv_sem,
+    *more,
 ):
     X, Y, Z, L = shape = phi.shape
     me = {axis: lax.axis_index(axis) for axis in AXES}
@@ -122,6 +142,8 @@
         wide[d, :, :L] = rounded
         sums = jnp.sum(rounded.astype(F32), axis=1, keepdims=True)
         wide[d, :, L:] = jnp.broadcast_to(sums, (L, L)).astype(BF16)
+
+    mean[...] = jnp.full((L, L), 1.0 / L, BF16)
 
     N = Halo(nx, ny, nz, nzh, nzo, True, shape)
     A = Halo(ax, ay, az, azh, azo, False, shape)
@@ -148,8 +170,10 @@
             plan.append((sends, gets, copy))
         return plan
 
-    def start(plan, field, value):
-        for d, (sends, gets, copy) in enumerate(plan):
+    def start(plan, field, value, which):
+        for d in which:
+            sends, gets, copy = plan[d]
+
             @pl.when(sends)
             def _():
                 copy.start()
@@ -171,27 +195,32 @@
             def _():
                 copy.wait_send()
 
-    def columns(lo, hi, step):
+    def planes(lo, hi, step, stride=1):
+        def one(x, carry):
+            step(x * stride)
+            return carry
+
+        lax.fori_loop(lo, hi, one, 0)
+
+    def columns(lo, hi, step, stride=1, width=1):
+        pieces = Y // width
+
         def one(i, carry):
-            step(i // Y, i % Y)
+            for j in range(width):
+                step((i // pieces) * stride, (i % pieces) * width + j)
             return carry
 
-        lax.fori_loop(lo * Y, hi * Y, one, 0)
-
-    def planes(lo, hi, step):
-        def one(x, carry):
-            step(x)
-            return carry
-
-        lax.fori_loop(lo, hi, one, 0)
+        lax.fori_loop(lo * pieces, hi * pieces, one, 0)
+
+    inside, rims = (1, X - 1), (0, 2)
 
     cuts = [pl.ds(c * CHUNK, CHUNK) for c in range(Z // CHUNK)]
     last = len(cuts) - 1
 
-    def send_terms(messages, shifted):
-        def hidden(x, y):
+    def hidden(messages, store, fresh):
+        def one(x, y):
             for cut in cuts:
-                if shifted:
+                if fresh:
                     potential = jnp.exp(unary[x, y, cut].astype(F32))
                     phi[x, y, cut] = potential
                 else:
@@ -199,33 +228,29 @@
                 fields = [messages[e, x, y, cut].astype(F32) for e in range(6)]
                 products = leave_one_out(potential, fields)
                 for e in range(6):
-                    hb[OPPOSE[e], x, y, cut] = products[e].astype(BF16)
-
-        columns(0, X, hidden)
-
-        def outgoing(x):
+                    store[OPPOSE[e], x, y, cut] = products[e].astype(BF16)
+
+        return one
+
+    def outgoing(store, scales, field, shifted):
+        def one(x):
             for d in range(6):
                 both = jnp.dot(
-                    hb[d, x].reshape(Y * Z, L), wide[d], preferred_element_type=F32
+                    store[d, x].reshape(Y * Z, L), wide[d], preferred_element_type=F32
                 )
                 scale = L * recip(both[:, L:])
-                inv[d, x] = scale.reshape(Y, Z, L)
+                scales[d, x] = scale.reshape(Y, Z, L)
                 normal = (both[:, :L] * scale).reshape(Y, Z, L)
-                if d < 2:
-                    nx[d, x + N.own(d)] = normal.astype(BF16)
-                elif d < 4:
-                    ny[d - 2, x, pl.ds(N.own(d), Y)] = normal.astype(BF16)
-                else:
-                    nz[d - 4, x] = normal.astype(BF16)
-                    if shifted:
-                        for y in range(Y):
-                            edge = Z - 1 if d == 4 else 0
-                            nzo[d - 4, pl.ds(x * Y + y, 1)] = normal[y, edge:edge + 1]
-                            nzs[d - 4, x, y] = pltpu.roll(
-                                normal[y], 1 if d == 4 else Z - 1, 0
-                            ).astype(BF16)
-
-        planes(0, X, outgoing)
+                field.plane(d, x)[...] = normal.astype(BF16)
+                if d >= 4 and shifted:
+                    for y in range(Y):
+                        edge = Z - 1 if d == 4 else 0
+                        nzo[d - 4, pl.ds(x * Y + y, 1)] = normal[y, edge:edge + 1]
+                        nzs[d - 4, x, y] = pltpu.roll(
+                            normal[y], 1 if d == 4 else Z - 1, 0
+                        ).astype(BF16)
+
+        return one
 
     def belief(x, y):
         spot = pl.ds(x * Y + y, 1)
@@ -258,10 +283,11 @@
                     azo[1, spot] = value[CHUNK - 1:CHUNK]
                 after = after * fields[e]
 
-    def grad_out(field):
+    def grad_out(field, local, scales):
         def one(x, y):
             row = lax.broadcasted_iota(jnp.int32, (Z, L), 0)
             spot = pl.ds(x * Y + y, 1)
+            grads, inners = [], []
             for d in range(6):
                 if d < 4:
                     grad = field.at_shifted(d, x, y)[...].astype(F32)
@@ -272,32 +298,31 @@
                         grad = jnp.where(row == Z - 1, halo, pltpu.roll(value, Z - 1, 0))
                     else:
                         grad = jnp.where(row == 0, halo, pltpu.roll(value, 1, 0))
-                place = N.at_own(d, x, y)
-                inner = jnp.sum(grad * place[...].astype(F32), axis=-1, keepdims=True) * (1.0 / L)
-                place[...] = (inv[d, x, y] * (grad - inner)).astype(BF16)
+                part = (grad * local.at_own(d, x, y)[...].astype(F32)).astype(BF16)
+                grads.append(grad)
+                inners.append(jnp.dot(part, mean[...], preferred_element_type=F32))
+            for d in range(6):
+                local.at_own(d, x, y)[...] = (
+                    scales[d, x, y] * (grads[d] - inners[d])
+                ).astype(BF16)
 
         return one
 
-    def go_plane(d, x):
-        if d < 2:
-            value = nx[d, x + N.own(d)]
-        elif d < 4:
-            value = ny[d - 2, x, pl.ds(N.own(d), Y)]
-        else:
-            value = nz[d - 4, x]
-        return value.reshape(Y * Z, L)
-
-    def weight_terms(x):
-        for d in range(6):
-            acc[d] += lax.dot_general(
-                hb[d, x].reshape(Y * Z, L), go_plane(d, x), (((0,), (0,)), ((), ())),
-                preferred_element_type=F32,
-            )
-
-    def hidden_terms(x):
+    def weight_terms(store, local):
+        def one(x):
+            for d in range(6):
+                acc[d] += lax.dot_general(
+                    store[d, x].reshape(Y * Z, L), local.plane(d, x)[...].reshape(Y * Z, L),
+                    (((0,), (0,)), ((), ())), preferred_element_type=F32,
+                )
+
+        return one
+
+    def hidden_terms(x, local):
         for d in range(6):
             hidden_grad[d] = lax.dot_general(
-                go_plane(d, x), psib[d], (((1,), (1,)), ((), ())), preferred_element_type=F32
+                local.plane(d, x)[...].reshape(Y * Z, L), psib[d], (((1,), (1,)), ((), ())),
+                preferred_element_type=F32,
             ).reshape(Y, Z, L)
 
     def adjoint(messages, field):
@@ -334,43 +359,64 @@
 
         return one
 
+    if early:
+        hb_one, inv_one = more[0], more[1]
+        local_one = Flat(more[2])
+    else:
+        hb_one, inv_one, local_one = hb, inv, N
+    acc[...] = jnp.zeros_like(acc)
     loads[0].wait()
     loads[1].wait()
-    send_terms(second, True)
+    one = exchange(N, 0)
+    columns(*rims, hidden(second, hb, True), stride=X - 1)
+    planes(*rims, outgoing(hb, inv, N, True), stride=X - 1)
     pl.semaphore_wait(barrier, group + others - 2)
-    one = exchange(N, 0)
-    start(one, N, 1.0)
-    acc[...] = jnp.zeros_like(acc)
+    start(one, N, 1.0, range(2))
+    columns(*inside, hidden(second, hb, True))
+    planes(*inside, outgoing(hb, inv, N, True))
+    start(one, N, 1.0, range(2, 6))
+    loads[3].wait()
+    if early:
+        columns(0, X, hidden(first, hb_one, False))
     loads[2].wait()
-    wait_recv(one)
-    columns(0, X, belief)
+    wait_recv(one[2:])
+    columns(*inside, belief, width=2)
+    wait_recv(one[:2])
+    columns(*rims, belief, stride=X - 1, width=2)
     two = exchange(A, 1)
-    start(two, A, 0.0)
+    start(two, A, 0.0, range(6))
+    if early:
+        planes(0, X, outgoing(hb_one, inv_one, local_one, False))
     wait_send(one)
-    wait_recv(two)
 
     def second_back(x):
-        each = grad_out(A)
+        each = grad_out(A, N, inv)
         lax.fori_loop(0, Y, lambda y, carry: (each(x, y), carry)[1], 0)
-        weight_terms(x)
-        hidden_terms(x)
+        hidden_terms(x, N)
         combine = adjoint(second, B)
         lax.fori_loop(0, Y, lambda y, carry: (combine(x, y), carry)[1], 0)
 
-    planes(0, X, second_back)
+    wait_recv(two[2:])
+    planes(*inside, second_back)
+    wait_recv(two[:2])
+    planes(*rims, second_back, stride=X - 1)
     three = exchange(B, 2)
-    start(three, B, 0.0)
+    start(three, B, 0.0, range(6))
+    planes(0, X, weight_terms(hb, N))
     wait_send(two)
 
-    loads[3].wait()
-    send_terms(first, False)
-    wait_recv(three)
-    columns(0, X, grad_out(B))
-    planes(0, X, weight_terms)
+    if not early:
+        columns(0, X, hidden(first, hb_one, False))
+        planes(0, X, outgoing(hb_one, inv_one, local_one, False))
+    wait_recv(three[2:])
+    columns(*inside, grad_out(B, local_one, inv_one))
+    wait_recv(three[:2])
+    columns(*rims, grad_out(B, local_one, inv_one), stride=X - 1)
+    planes(0, X, weight_terms(hb_one, local_one))
     wait_send(three)
 
     def first_back(x):
-        hidden_terms(x)
+        hidden_terms(x, local_one)
         combine = adjoint(first, None)
         lax.fori_loop(0, Y, lambda y, carry: (combine(x, y), carry)[1], 0)
 
@@ -443,6 +489,12 @@
     others = sizes[other]
     rows = 6 * L // group
     field = (X, Y, Z, L)
+    early = X * Y * Z * L <= 384 * 1024
+    more = [
+        pltpu.VMEM((6,) + field, BF16),
+        pltpu.VMEM((6,) + field, F32),
+        pltpu.VMEM((6,) + field, BF16),
+    ] if early else []
 
     def halo_set(extra):
         return [
@@ -453,7 +505,7 @@
 
     dma = pltpu.SemaphoreType.DMA
     return pl.pallas_call(
-        functools.partial(kernel, sizes, scatter, other),
+        functools.partial(kernel, early, sizes, scatter, other),
         out_shape=(
             jax.ShapeDtypeStruct(field, F32),
             jax.ShapeDtypeStruct((6, L, L), F32),
@@ -488,6 +540,7 @@
             pltpu.VMEM((group - 1, rows, L), BF16),
             pltpu.VMEM((others, rows, L), BF16),
             pltpu.VMEM((group, rows, L), BF16),
+            pltpu.VMEM((L, L), BF16),
             dma((5,)),
             dma((3, 6)),
             dma((3, 6)),
@@ -497,7 +550,8 @@
             dma((others - 1,)),
             dma((group - 1,)),
             dma((group - 1,)),
-        ],
+        ]
+        + more,
         compiler_params=pltpu.CompilerParams(
             collective_id=0, has_side_effects=True, vmem_limit_bytes=64 * 1024 * 1024 - 65536
         ),

time: 57.8 us -> 58.9 us (1.019)
  Pallas kernels: 52.9 us -> 54 us
    pallas_call x1, Pallas kernels: 52.9 us -> 54 us  [body(): pl.pallas_call(functools.partial(kernel, early, sizes, scatter, other), o...]
where the time goes in v2:
time: 58.9 us; the launch traced here: 58.7 us
  Pallas kernels  54 us (92%)
  local copies, waits for them, and re-layouts  4.07 us (7%)
  between operations  0.64 us (1%)
    pallas_call x1, Pallas kernels, body(): pl.pallas_call(functools.partial(kernel, early, sizes, scatter, other), o...  54 us
    unnamed x2, local copies, waits for them, and re-layouts  4.07 us

profile of v2, /device:TPU:0, one launch (start us, length us, event | category | flops | bytes accessed | tf_op | source)
XLA Modules:
  0.0 58.7 jit_solution(2440090021735213674)
XLA Ops:
  0.6 54.0 %shard_map.68 = (f32[4,8,64,128]{3,2,1,0:T(8,128)}, f32[6,128,128]{2,1,0:T(8,128)}) custom-call(bf16[4,8,64,128]{3,2,1,0:T(8,128)(2,1)} %unary_h.1, f32[6,128,128]{2,1,0:T(8,128)} %compat.1, bf16[6,4,8,64,128]{4,3,2,1,0:T(8,128)(2,1)} %first_h.1, bf16[6,4,8,64,128]{4,3,2,1,0:T(8,128)(2,1)} %second_h.1, f32[4,8,64,128]{3,2,1,0:T(8,128)} %cot_h.1), custom_call_target="tpu_custom_call" | custom-call | tf_op jit(solution)/shard_map/pallas_call | solution.py:507
  54.6 2.3 %copy.9 = f32[4,8,64,128]{3,2,1,0:T(8,128)} copy(f32[4,8,64,128]{3,2,1,0:T(8,128)} %get-tuple-element.4) | data formatting | bytes 2097152
  56.9 1.8 %copy.10 = f32[6,128,128]{2,1,0:T(8,128)} copy(f32[6,128,128]{2,1,0:T(8,128)} %get-tuple-element.5) | data formatting | bytes 786432

commit v3 on v2

--- a/solution.py
+++ b/solution.py
@@ -284,27 +284,28 @@
                 after = after * fields[e]
 
     def grad_out(field, local, scales):
-        def one(x, y):
+        def one(x):
             row = lax.broadcasted_iota(jnp.int32, (Z, L), 0)
-            spot = pl.ds(x * Y + y, 1)
-            grads, inners = [], []
-            for d in range(6):
-                if d < 4:
-                    grad = field.at_shifted(d, x, y)[...].astype(F32)
+            for d in (0, 2, 4, 1, 3, 5):
+                if d < 2:
+                    grad = field.x[d, x + field.read(d)].astype(F32)
+                elif d < 4:
+                    grad = field.y[d - 2, x, pl.ds(field.read(d), Y)].astype(F32)
                 else:
-                    value = field.z[d - 4, x, y].astype(F32)
-                    halo = field.zhalo[d - 4, spot]
-                    if d == 4:
-                        grad = jnp.where(row == Z - 1, halo, pltpu.roll(value, Z - 1, 0))
-                    else:
-                        grad = jnp.where(row == 0, halo, pltpu.roll(value, 1, 0))
-                part = (grad * local.at_own(d, x, y)[...].astype(F32)).astype(BF16)
-                grads.append(grad)
-                inners.append(jnp.dot(part, mean[...], preferred_element_type=F32))
-            for d in range(6):
-                local.at_own(d, x, y)[...] = (
-                    scales[d, x, y] * (grads[d] - inners[d])
-                ).astype(BF16)
+                    grad = []
+                    for y in range(Y):
+                        value = field.z[d - 4, x, y].astype(F32)
+                        halo = field.zhalo[d - 4, pl.ds(x * Y + y, 1)]
+                        if d == 4:
+                            grad.append(jnp.where(row == Z - 1, halo, pltpu.roll(value, Z - 1, 0)))
+                        else:
+                            grad.append(jnp.where(row == 0, halo, pltpu.roll(value, 1, 0)))
+                    grad = jnp.stack(grad)
+                part = (grad * local.plane(d, x)[...].astype(F32)).astype(BF16)
+                inner = jnp.dot(
+                    part.reshape(Y * Z, L), mean[...], preferred_element_type=F32
+                ).reshape(Y, Z, L)
+                local.plane(d, x)[...] = (scales[d, x] * (grad - inner)).astype(BF16)
 
         return one
 
@@ -390,8 +391,7 @@
     wait_send(one)
 
     def second_back(x):
-        each = grad_out(A, N, inv)
-        lax.fori_loop(0, Y, lambda y, carry: (each(x, y), carry)[1], 0)
+        grad_out(A, N, inv)(x)
         hidden_terms(x, N)
         combine = adjoint(second, B)
         lax.fori_loop(0, Y, lambda y, carry: (combine(x, y), carry)[1], 0)
@@ -409,9 +409,9 @@
         columns(0, X, hidden(first, hb_one, False))
         planes(0, X, outgoing(hb_one, inv_one, local_one, False))
     wait_recv(three[2:])
-    columns(*inside, grad_out(B, local_one, inv_one))
+    planes(*inside, grad_out(B, local_one, inv_one))
     wait_recv(three[:2])
-    columns(*rims, grad_out(B, local_one, inv_one), stride=X - 1)
+    planes(*rims, grad_out(B, local_one, inv_one), stride=X - 1)
     planes(0, X, weight_terms(hb_one, local_one))
     wait_send(three)
 

time: 58.9 us -> 49.5 us (0.84)
  Pallas kernels: 54 us -> 44.6 us
    pallas_call x1, Pallas kernels: 54 us -> 44.6 us  [body(): pl.pallas_call(functools.partial(kernel, early, sizes, scatter, other), o...]
where the time goes in v3:
time: 49.5 us; the launch traced here: 49.3 us
  Pallas kernels  44.6 us (90%)
  local copies, waits for them, and re-layouts  4.07 us (8%)
  between operations  0.64 us (1%)
    pallas_call x1, Pallas kernels, body(): pl.pallas_call(functools.partial(kernel, early, sizes, scatter, other), o...  44.6 us
    unnamed x2, local copies, waits for them, and re-layouts  4.07 us

profile of v3, /device:TPU:0, one launch (start us, length us, event | category | flops | bytes accessed | tf_op | source)
XLA Modules:
  0.0 49.3 jit_solution(5763328719580557868)
XLA Ops:
  0.6 44.6 %shard_map.68 = (f32[4,8,64,128]{3,2,1,0:T(8,128)}, f32[6,128,128]{2,1,0:T(8,128)}) custom-call(bf16[4,8,64,128]{3,2,1,0:T(8,128)(2,1)} %unary_h.1, f32[6,128,128]{2,1,0:T(8,128)} %compat.1, bf16[6,4,8,64,128]{4,3,2,1,0:T(8,128)(2,1)} %first_h.1, bf16[6,4,8,64,128]{4,3,2,1,0:T(8,128)(2,1)} %second_h.1, f32[4,8,64,128]{3,2,1,0:T(8,128)} %cot_h.1), custom_call_target="tpu_custom_call" | custom-call | tf_op jit(solution)/shard_map/pallas_call | solution.py:507
  45.2 2.3 %copy.9 = f32[4,8,64,128]{3,2,1,0:T(8,128)} copy(f32[4,8,64,128]{3,2,1,0:T(8,128)} %get-tuple-element.4) | data formatting | bytes 2097152
  47.5 1.8 %copy.10 = f32[6,128,128]{2,1,0:T(8,128)} copy(f32[6,128,128]{2,1,0:T(8,128)} %get-tuple-element.5) | data formatting | bytes 786432
